TPU v7x, 256 devices: a whole 4x4x8 slice. The times are simulated.
256 devices in a mesh: seq: 64 (over x, z, core), vocab: 4 (over y).
Axes of the slice: x: 4, y: 4, z: 8, core: 2. Of those that a mesh axis runs over, the one named last changes fastest.
Arguments:
- query: bfloat16 [8192, 64, 576], P('seq', 'vocab'), may hold values from -150 to 150
- latent_cache: bfloat16 [512, 64, 576], P('seq'), may hold values from -4 to 4
- block_lists: int32 [512, 16], P('seq'), may hold values from -1 to 511, as said below
- d_out: bfloat16 [8192, 64, 512], P('seq', 'vocab'), may hold values from -3 to 3
Outputs:
- grad_query: bfloat16 [8192, 64, 576], P('seq', 'vocab')
- grad_cache: float32 [512, 64, 576], P('seq', 'vocab')
Inputs may be any that keep to these rules, and one draw needn't show every extreme that they name: `block_lists`: list j serves query rows j * 16 to j * 16 + 15. Its first entry is the block that holds those rows; the others are distinct blocks before it, followed by -1 entries that select nothing. The lists of one device's 128 rows name at most 2 distinct blocks held by any one other device, and exactly 2 held by some device, on every device but the first.
All inputs are finite; a program needn't handle non-finite values.
Results may differ from a plain program's by a relative error of at most 0.006.
Values may be sent and summed in bfloat16 or wider, within the bound.
No kernel may reach another device: no remote copies, remote signals or barrier semaphores. Data moves between devices by JAX's collectives and lax.ppermute only.
A program may use at most 192 MiB of HBM per device.

v0:
```python
import jax
import jax.numpy as jnp
from jax import lax
from jax.sharding import PartitionSpec as P

CAP = 2


score_scale = 0.07216878364870323


def receive_into(own, arrived, incoming):
    slots = incoming.reshape(-1)
    onehot = (slots[:, None] == jnp.arange(own.shape[0], dtype=jnp.int32)[None, :]).astype(
        jnp.float32
    )
    flat = arrived.reshape(slots.shape[0], -1)
    added = jnp.einsum(
        "nb,nf->bf",
        onehot,
        flat,
        precision=lax.Precision.HIGHEST,
        preferred_element_type=jnp.float32,
    )
    return own + added.reshape(own.shape)


def body(query, latent_cache, block_lists, d_out):
    shard = lax.axis_index("seq")
    shards = lax.axis_size("seq")
    per_shard = latent_cache.shape[0]
    block_len = latent_cache.shape[1]
    latent = latent_cache.shape[2]
    rows = query.shape[0]
    heads = query.shape[1]
    value_rows = d_out.shape[2]
    groups = block_lists.shape[0]
    qgroup = rows // groups
    select = block_lists.shape[1]
    first_block = shard * per_shard
    owner = jnp.where(block_lists >= 0, block_lists // per_shard, -1)
    remote = (block_lists >= 0) & (owner != shard)
    every_block = jnp.arange(shards * per_shard, dtype=jnp.int32)
    matches = block_lists.reshape(-1)[:, None] == every_block[None, :]
    present = (
        jnp.any(matches & remote.reshape(-1)[:, None], axis=0)
        .astype(jnp.int32)
        .reshape(shards, per_shard)
    )
    rank = jnp.cumsum(present, axis=1)
    wanted_rank = jnp.arange(1, CAP + 1, dtype=jnp.int32)[None, :, None]
    slot_hit = present[:, None, :] * (rank[:, None, :] == wanted_rank).astype(jnp.int32)
    requests = (
        jnp.sum(slot_hit * jnp.arange(per_shard, dtype=jnp.int32)[None, None, :], axis=2)
        + jnp.sum(slot_hit, axis=2)
        - 1
    )
    incoming = lax.all_to_all(requests, "seq", split_axis=0, concat_axis=0, tiled=True)
    wanted = jnp.maximum(incoming, 0)
    fetched = lax.all_to_all(latent_cache[wanted], "seq", split_axis=0, concat_axis=0, tiled=True)
    table = jnp.concatenate(
        [latent_cache, fetched.reshape(shards * CAP, block_len, latent)], axis=0
    )
    slot_rank = jnp.sum(matches.astype(jnp.int32) * rank.reshape(-1)[None, :], axis=1).reshape(
        groups, select
    )
    table_index = jnp.where(
        owner == shard, block_lists - first_block, per_shard + owner * CAP + slot_rank - 1
    )
    table_index = jnp.where(block_lists >= 0, table_index, 0)
    shard_offset = per_shard * block_len - rows
    query_pos = (
        shard * per_shard * block_len + shard_offset + jnp.arange(rows, dtype=jnp.int32)
    ).reshape(groups, qgroup)

    def one_group(inputs):
        query_group, output_group, index_group, block_group, position_group = inputs
        key_rows = table[index_group]
        scores = (
            jnp.einsum("rhl,skl->rhsk", query_group, key_rows, preferred_element_type=jnp.float32)
            * score_scale
        )
        grad_probs = jnp.einsum(
            "bta,zca->btzc",
            output_group,
            key_rows[:, :, :value_rows],
            preferred_element_type=jnp.float32,
        )
        key_pos = block_group[:, None] * block_len + jnp.arange(block_len, dtype=jnp.int32)[None, :]
        allowed = (block_group[:, None] >= 0)[None, :, :] & (
            key_pos[None, :, :] <= position_group[:, None, None]
        )
        allowed = allowed[:, None, :, :]
        masked = jnp.where(allowed, scores, -jnp.inf)
        top = jnp.max(masked, axis=(2, 3), keepdims=True)
        expo = jnp.exp(masked - top)
        probs = expo / jnp.sum(expo, axis=(2, 3), keepdims=True)
        delta = jnp.sum(probs * grad_probs, axis=(2, 3), keepdims=True)
        probability_lower = probs.astype(jnp.bfloat16)
        grad_low = (score_scale * probs * (grad_probs - delta)).astype(jnp.bfloat16)
        grad_query = jnp.einsum(
            "rhsk,skl->rhl", grad_low, key_rows, preferred_element_type=jnp.float32
        ).astype(jnp.bfloat16)
        grad_keys = jnp.einsum(
            "rhsk,rhl->skl", grad_low, query_group, preferred_element_type=jnp.float32
        )
        grad_values = jnp.einsum(
            "adty,ade->tye", probability_lower, output_group, preferred_element_type=jnp.float32
        )
        grad_keys = grad_keys + jnp.pad(grad_values, ((0, 0), (0, 0), (0, latent - value_rows)))
        return (grad_query, grad_keys)

    grad_query, grad_keys = lax.map(
        one_group,
        (
            query.reshape(groups, qgroup, heads, latent),
            d_out.reshape(groups, qgroup, heads, value_rows),
            table_index,
            block_lists,
            query_pos,
        ),
    )
    table_grad = jnp.zeros((per_shard + shards * CAP, block_len, latent), jnp.float32)
    table_grad = table_grad.at[table_index.reshape(-1)].add(
        grad_keys.reshape(-1, block_len, latent)
    )
    local_grad = table_grad[:per_shard]
    remote_grad = table_grad[per_shard:].reshape(shards, CAP, block_len, latent)
    arrived = lax.all_to_all(
        remote_grad.astype(jnp.bfloat16), "seq", split_axis=0, concat_axis=0, tiled=True
    ).astype(remote_grad.dtype)
    owned = receive_into(local_grad, arrived, incoming)
    grad_cache = lax.psum_scatter(owned, "vocab", scatter_dimension=1, tiled=True)
    return (grad_query.reshape(rows, heads, latent), grad_cache)


def solution(mesh):
    in_specs = (
        P("seq", "vocab", None),
        P("seq", None, None),
        P("seq", None),
        P("seq", "vocab", None),
    )
    out_specs = (P("seq", "vocab", None), P("seq", "vocab", None))
    return jax.shard_map(body, mesh=mesh, in_specs=in_specs, out_specs=out_specs, check_vma=False)
```

profile of v0, /device:TPU:2, one launch (start us, length us, event | category | flops | bytes accessed | tf_op | source)
XLA Modules:
  0.0 804.5 jit_solution(17605344303485273916)
XLA Ops:
  9.5 20.4 %all_to_all.16 = s32[64,1,2]{2,1,0:T(1,128)S(1)} all-to-all(s32[64,1,2]{2,1,0:T(1,128)S(1)} %copy.35), channel_id=1, replica_groups=mesh['seq'=64,'vocab'=4] {'seq'}, dimensions={0} | all-to-all | bytes 1024 | tf_op jit(solution)/shard_map/all_to_all | solution.py:58
  31.4 8.8 %gather_fusion.1 = bf16[128,64,576]{2,1,0:T(8,128)(2,1)} fusion(bf16[8,64,576]{2,1,0:T(8,128)(2,1)} %param.7, s32[1024]{0:T(1024)S(1)} %pad_clamp_fusion.1), kind=kCustom, calls=%fused_computation.1 | custom fusion | bytes 18874880 | tf_op jit(solution)/shard_map/gather | solution.py:60
  40.2 6.7 all-to-all-start.1
  47.4 3.5 copy.32
  50.9 225.5 %all-to-all-done.1 = bf16[64,2,64,576]{3,2,1,0:T(8,128)(2,1)} async-done(((bf16[64,2,64,576]{3,2,1,0:T(8,128)(2,1)}), bf16[64,2,64,576]{3,2,1,0:T(8,128)(2,1)}, u32[]{:S(2)}, u32[]{:S(2)}) %all-to-all-start.1) | async-done | bytes 9437216 | tf_op jit(solution)/shard_map/all_to_all | solution.py:60
  276.5 10.9 %pad_maximum_fusion = bf16[136,64,576]{2,1,0:T(8,128)(2,1)} fusion(bf16[128,64,576]{2,1,0:T(8,128)(2,1)} %bitcast.24, bf16[8,64,576]{2,1,0:T(8,128)(2,1)S(1)} %copy-done), kind=kLoop, calls=%fused_computation.49 | loop fusion | flops 5013504 | bytes 20054016 | tf_op jit(solution)/shard_map/concatenate | solution.py:61
  287.3 139.1 %while.14 = (s32[]{:T(128)}, bf16[8,16,16,576]{3,2,1,0:T(8,128)(2,1)}, f32[8,16,64,576]{3,2,1,0:T(8,128)}, s32[8,16]{1,0:T(8,128)S(1)}, s32[8,16]{1,0:T(8,128)S(...) while((s32[]{:T(128)}, ...), condition=%wide.region_9.10_spmd, body=%wide.region_5.9_spmd.sunk | while | flops 1450427776 | bytes 24206184 | solution.py:113
  287.6 4.9 gather_fusion
  292.5 2.1 fusion.70
  295.3 1.9 convolution_bitcast_fusion.2
  297.2 2.0 multiply_reduce_fusion.2
  301.5 3.2 bitcast_dynamic-update-slice_fusion.2
  305.0 4.9 gather_fusion
  309.9 2.1 fusion.70
  312.7 1.9 convolution_bitcast_fusion.2
  314.6 2.0 multiply_reduce_fusion.2
  317.5 1.4 fusion.72
  318.9 3.2 bitcast_dynamic-update-slice_fusion.2
  322.3 4.9 gather_fusion
  327.3 2.1 fusion.70
  330.1 1.9 convolution_bitcast_fusion.2
  332.0 2.0 multiply_reduce_fusion.2
  334.9 1.4 fusion.72
  336.3 3.3 bitcast_dynamic-update-slice_fusion.2
  339.8 4.9 gather_fusion
  344.8 2.1 fusion.70
  347.5 1.9 convolution_bitcast_fusion.2
  349.5 2.0 multiply_reduce_fusion.2
  352.4 1.4 fusion.72
  353.8 3.2 bitcast_dynamic-update-slice_fusion.2
  357.2 4.9 gather_fusion
  362.2 2.1 fusion.70
  365.0 1.9 convolution_bitcast_fusion.2
  366.9 2.0 multiply_reduce_fusion.2
  369.8 1.4 fusion.72
  371.2 3.2 bitcast_dynamic-update-slice_fusion.2
  374.6 4.9 gather_fusion
  379.5 2.1 fusion.70
  382.3 1.9 convolution_bitcast_fusion.2
  384.2 2.0 multiply_reduce_fusion.2
  388.5 3.2 bitcast_dynamic-update-slice_fusion.2
  391.9 4.9 gather_fusion
  396.9 2.1 fusion.70
  399.7 1.9 convolution_bitcast_fusion.2
  401.6 2.0 multiply_reduce_fusion.2
  404.5 1.4 fusion.72
  405.9 3.2 bitcast_dynamic-update-slice_fusion.2
  409.3 4.9 gather_fusion
  414.2 2.1 fusion.70
  417.0 1.9 convolution_bitcast_fusion.2
  418.9 2.0 multiply_reduce_fusion.2
  423.2 3.2 bitcast_dynamic-update-slice_fusion.2
  426.5 10.2 %broadcast_in_dim.65 = f32[136,64,576]{2,1,0:T(8,128)} broadcast(f32[]{:T(128)} %constant.101.clone.1), dimensions={} | broadcast | bytes 20054020 | tf_op jit(solution)/shard_map/broadcast_in_dim | solution.py:123
  436.7 45.0 %scatter_fusion = f32[136,64,576]{2,1,0:T(8,128)} fusion(f32[136,64,576]{2,1,0:T(8,128)} %broadcast_in_dim.65, s32[128]{0:T(128)S(1)} %fusion.46, f32[128,64,576]{2,1,0:T(8,128)} %bitcast.136), kind=kCustom, calls=%fused_computation.2 | custom fusion | flops 4718592 | bytes 56623616 | tf_op jit(solution)/shard_map/scatter-add | solution.py:124
  481.6 12.8 %slice.25 = bf16[128,64,576]{2,1,0:T(8,128)(2,1)} slice(f32[136,64,576]{2,1,0:T(8,128)} %scatter_fusion), slice={[8:136], [0:64], [0:576]} | slice | bytes 18874368 | tf_op jit(solution)/shard_map/slice | solution.py:128
  494.5 7.6 all-to-all-start.2
  502.5 1.4 slice.20
  503.9 227.7 %all-to-all-done.2 = bf16[64,2,64,576]{3,2,1,0:T(8,128)(2,1)} async-done(((bf16[64,2,64,576]{3,2,1,0:T(8,128)(2,1)}), bf16[64,2,64,576]{3,2,1,0:T(8,128)(2,1)}, u32[]{:S(2)}, u32[]{:S(2)}) %all-to-all-start.2) | async-done | bytes 9437216 | tf_op jit(solution)/shard_map/all_to_all | solution.py:129
  731.6 18.5 %reshape.207 = bf16[128,36864]{1,0:T(8,128)(2,1)} reshape(bf16[64,2,64,576]{3,2,1,0:T(8,128)(2,1)} %all-to-all-done.2) | data formatting | bytes 18874368 | tf_op jit(solution)/shard_map/reshape | solution.py:17
  750.1 12.5 %copy.37 = bf16[36864,128]{1,0:T(8,128)(2,1)} copy(bf16[36864,128]{0,1:T(8,128)(2,1)} %bitcast.135) | data formatting | bytes 18874368 | tf_op jit(solution)/shard_map/nb,nf->bf/dot_general | solution.py:18
  762.6 7.9 convolution_add_fusion
  770.5 4.7 copy.38
  775.2 20.7 %reduce-scatter.2.cloned.1.call-done = f32[8,16,576]{2,0,1:T(8,128)} async-done(((f32[8,64,576]{2,0,1:T(8,128)}), f32[8,16,576]{2,0,1:T(8,128)}) %reduce-scatter.2.cloned.1.call-update) | async-done | bytes 294928 | tf_op jit(solution)/shard_map/reduce_scatter | solution.py:133
  795.9 1.8 copy.39
  (101 shorter events, 23.0 us)
Async XLA Ops:
  40.2 7.1 copy-start.2
  40.2 7.2 copy-start.1
  40.2 236.2 %all-to-all-start.1 = ((bf16[64,2,64,576]{3,2,1,0:T(8,128)(2,1)}), bf16[64,2,64,576]{3,2,1,0:T(8,128)(2,1)}, u32[]{:S(2)}, u32[]{:S(2)}) async-start(bf16[64,2,64,576]{3,2,1,0:T(8,128)(2,1)} %bitcast.132), calls=%async_computation.1 | async-start | bytes 20971520 | tf_op jit(solution)/shard_map/all_to_all | solution.py:60
  47.4 229.1 %copy-start = (bf16[8,64,576]{2,1,0:T(8,128)(2,1)S(1)}, bf16[8,64,576]{2,1,0:T(8,128)(2,1)}, u32[]{:S(2)}) copy-start(bf16[8,64,576]{2,1,0:T(8,128)(2,1)} %param.7) | copy-start | bytes 1769476
  494.5 237.1 %all-to-all-start.2 = ((bf16[64,2,64,576]{3,2,1,0:T(8,128)(2,1)}), bf16[64,2,64,576]{3,2,1,0:T(8,128)(2,1)}, u32[]{:S(2)}, u32[]{:S(2)}) async-start(bf16[64,2,64,576]{3,2,1,0:T(8,128)(2,1)} %bitcast.133), calls=%async_computation.2 | async-start | bytes 20971520 | tf_op jit(solution)/shard_map/all_to_all | solution.py:129
  502.1 293.9 %reduce-scatter.2.cloned.1.call-start = ((), (), s32[]{:S(2)}) async-start(), calls=%async_computation.4 | async-start | bytes 1638400 | tf_op jit(solution)/shard_map/reduce_scatter | solution.py:133
Sparse Core Ops, SparseCore 0:
  770.6 25.2 reduce-scatter.1
where the time goes:
time: 807 us; the launch traced here: 805 us
  waiting for transfers between devices  474 us (59%)
  local copies, waits for them, and re-layouts  116 us (14%)
  matrix products  92.8 us (11%)
  other arithmetic  72.2 us (9%)
  blocking collectives  20.4 us (3%)
  starting transfers between devices  14.5 us (2%)
  between operations  14.2 us (2%)
    all_to_all x1, waiting for transfers between devices, body(): lax.all_to_all(remote_grad.astype(jnp.bfloat16), 'seq', split_axis=0, con...  228 us
    all_to_all x1, waiting for transfers between devices, body(): lax.all_to_all(latent_cache[wanted], 'seq', split_axis=0, concat_axis=0,...  226 us
    scatter-add x1, other arithmetic, body(): table_grad.at[table_index.reshape(-1)]  45 us
    gather x8, local copies, waits for them, and re-layouts, one_group(): key_rows = table[index_group]  39.6 us
    dot_general x8, matrix products, one_group(): jnp.einsum('rhsk,rhl->skl', grad_low, query_group, preferred_element_type...  25.6 us
    reduce_scatter x1, waiting for transfers between devices, body(): lax.psum_scatter(owned, 'vocab', scatter_dimension=1, tiled=True)  20.7 us
    all_to_all x1, blocking collectives, body(): lax.all_to_all(requests, 'seq', split_axis=0, concat_axis=0, tiled=True)  20.4 us
    reshape x1, local copies, waits for them, and re-layouts, receive_into(): flat = arrived.reshape(slots.shape[0], -1)  18.5 us
  transfers between devices with their start and end apart: 3, of which 3 were waited for; matrix products, arithmetic and copies ran while one was open for 1% of the time, Pallas kernels for 0%

commit v1 on v0

v1 whole, which is shorter than its diff:
```python
import functools

import jax
import jax.numpy as jnp
from jax import lax
from jax.experimental import pallas as pl
from jax.experimental.pallas import tpu as pltpu
from jax.sharding import PartitionSpec as P

CAP = 2
SCALE = 0.07216878364870323
LOG2E = 1.4426950408889634


def attention_kernel(start_ref, first_ref, q_ref, d_ref, k_ref, gq_ref, gk_ref, acc_ref):
    group = pl.program_id(0)
    tile = pl.program_id(1)
    parts, entries, part_len, latent = k_ref.shape
    keys_n = parts * entries * part_len
    rows, heads = q_ref.shape[1], q_ref.shape[2]
    cols = rows * heads
    value = d_ref.shape[3]
    q = q_ref[0].reshape(cols, latent)
    d = d_ref[0].reshape(cols, value)
    keys = k_ref[...].reshape(keys_n, latent)
    nt = (((1,), (1,)), ((), ()))
    scores = lax.dot_general(keys, q, nt, preferred_element_type=jnp.float32)
    grad_probs = lax.dot_general(keys[:, :value], d, nt, preferred_element_type=jnp.float32)

    shape = (part_len, cols)
    row = lax.broadcasted_iota(jnp.int32, shape, 1) // heads
    limit = first_ref[0] + group * rows + row - lax.broadcasted_iota(jnp.int32, shape, 0)
    strips = []
    for i in range(parts * entries):
        strip = scores[i * part_len : (i + 1) * part_len]
        strips.append(jnp.where(start_ref[group, i] <= limit, strip, -jnp.inf))
    masked = jnp.concatenate(strips, axis=0)
    top = jnp.max(masked, axis=0, keepdims=True)
    expo = jnp.exp2((masked - top) * (SCALE * LOG2E))
    inverse = 1.0 / jnp.sum(expo, axis=0, keepdims=True)
    delta = jnp.sum(expo * grad_probs, axis=0, keepdims=True) * inverse
    probs_low = (expo * inverse).astype(jnp.bfloat16)
    grad_low = (expo * (inverse * SCALE) * (grad_probs - delta)).astype(jnp.bfloat16)

    gq = lax.dot_general(grad_low, keys, (((0,), (0,)), ((), ())), preferred_element_type=jnp.float32)
    gq_ref[0] = gq.astype(jnp.bfloat16).reshape(rows, heads, latent)
    gk = jnp.dot(grad_low, q, preferred_element_type=jnp.float32)
    gv = jnp.dot(probs_low, d, preferred_element_type=jnp.float32)

    @pl.when(tile == 0)
    def _():
        acc_ref[...] = gk
        acc_ref[:, :value] += gv

    @pl.when(tile > 0)
    def _():
        acc_ref[...] += gk
        acc_ref[:, :value] += gv

    @pl.when(tile == pl.num_programs(1) - 1)
    def _():
        gk_ref[...] = acc_ref[...].astype(jnp.bfloat16).reshape(gk_ref.shape)


def attention(start, first, q, d, keys, groups):
    members, rows_all, heads, latent = q.shape
    value = d.shape[3]
    rows = rows_all // groups
    parts, entries_all, part_len, _ = keys.shape
    entries = entries_all // groups
    flops = 2 * members * rows_all * heads * parts * entries * part_len * (3 * latent + 2 * value)
    return pl.pallas_call(
        attention_kernel,
        grid_spec=pltpu.PrefetchScalarGridSpec(
            num_scalar_prefetch=2,
            grid=(groups, members),
            in_specs=[
                pl.BlockSpec((1, rows, heads, latent), lambda g, t, *_: (t, g, 0, 0)),
                pl.BlockSpec((1, rows, heads, value), lambda g, t, *_: (t, g, 0, 0)),
                pl.BlockSpec((parts, entries, part_len, latent), lambda g, t, *_: (0, g, 0, 0)),
            ],
            out_specs=[
                pl.BlockSpec((1, rows, heads, latent), lambda g, t, *_: (t, g, 0, 0)),
                pl.BlockSpec((parts, entries, part_len, latent), lambda g, t, *_: (0, g, 0, 0)),
            ],
            scratch_shapes=[pltpu.VMEM((parts * entries * part_len, latent), jnp.float32)],
        ),
        out_shape=[
            jax.ShapeDtypeStruct(q.shape, jnp.bfloat16),
            jax.ShapeDtypeStruct(keys.shape, jnp.bfloat16),
        ],
        compiler_params=pltpu.CompilerParams(
            dimension_semantics=("arbitrary", "arbitrary"), vmem_limit_bytes=50 * 1024 * 1024
        ),
        cost_estimate=pl.CostEstimate(flops=flops, bytes_accessed=16 << 20, transcendentals=1 << 21),
    )(start, first, q, d, keys)


def sum_by_block_kernel(index_ref, in_ref, local_ref, slots_ref, table_ref):
    table_ref[...] = jnp.zeros_like(table_ref)

    def add(i, carry):
        table_ref[index_ref[i]] += in_ref[i].astype(jnp.float32)
        return carry

    lax.fori_loop(0, in_ref.shape[0], add, 0)
    per = local_ref.shape[0]
    local_ref[...] = table_ref[:per]
    slots_ref[...] = table_ref[per:].astype(jnp.bfloat16)


def sum_by_block(index, entries, per_shard, slots):
    _, part_len, latent = entries.shape
    return pl.pallas_call(
        sum_by_block_kernel,
        in_specs=[pl.BlockSpec(memory_space=pltpu.SMEM), pl.BlockSpec(memory_space=pltpu.VMEM)],
        out_specs=[pl.BlockSpec(memory_space=pltpu.VMEM)] * 2,
        out_shape=[
            jax.ShapeDtypeStruct((per_shard, part_len, latent), jnp.float32),
            jax.ShapeDtypeStruct((slots, part_len, latent), jnp.bfloat16),
        ],
        scratch_shapes=[pltpu.VMEM((per_shard + slots, part_len, latent), jnp.float32)],
        compiler_params=pltpu.CompilerParams(vmem_limit_bytes=40 * 1024 * 1024),
        cost_estimate=pl.CostEstimate(flops=2 << 20, bytes_accessed=6 << 20, transcendentals=0),
    )(index, entries)


def receive_kernel(index_ref, in_ref, local_ref, out_ref, table_ref):
    per = local_ref.shape[0]
    table_ref[:per] = local_ref[...]

    def add(i, carry):
        table_ref[index_ref[i]] += in_ref[i].astype(jnp.float32)
        return carry

    lax.fori_loop(0, in_ref.shape[0], add, 0)
    out_ref[...] = table_ref[:per]


def receive(index, arrived, local):
    per, part_len, latent = local.shape
    return pl.pallas_call(
        receive_kernel,
        in_specs=[
            pl.BlockSpec(memory_space=pltpu.SMEM),
            pl.BlockSpec(memory_space=pltpu.VMEM),
            pl.BlockSpec(memory_space=pltpu.VMEM),
        ],
        out_specs=pl.BlockSpec(memory_space=pltpu.VMEM),
        out_shape=jax.ShapeDtypeStruct(local.shape, jnp.float32),
        scratch_shapes=[pltpu.VMEM((per + 1, part_len, latent), jnp.float32)],
        compiler_params=pltpu.CompilerParams(vmem_limit_bytes=40 * 1024 * 1024),
        cost_estimate=pl.CostEstimate(flops=2 << 20, bytes_accessed=4 << 20, transcendentals=0),
    )(index, arrived, local)


def body(query, latent_cache, block_lists, d_out):
    shard = lax.axis_index("seq")
    shards = lax.axis_size("seq")
    member = lax.axis_index("vocab")
    members = lax.axis_size("vocab")
    per_shard, block_len, latent = latent_cache.shape
    rows, heads, _ = query.shape
    value = d_out.shape[2]
    groups, select = block_lists.shape
    qgroup = rows // groups
    part_len = block_len // members
    groups_mine = groups // members
    slots = shards * CAP

    quarter = lax.dynamic_slice_in_dim(latent_cache, member * part_len, part_len, 1)
    table = lax.all_gather(quarter, "seq", axis=0, tiled=True)

    q = lax.all_to_all(
        query.reshape(members, rows // members, heads, latent), "vocab", 0, 0, tiled=True
    )
    d = lax.all_to_all(
        d_out.reshape(members, rows // members, heads, value), "vocab", 0, 0, tiled=True
    )

    flat = block_lists.reshape(-1)
    owner = jnp.where(flat >= 0, flat // per_shard, -1)
    remote = (flat >= 0) & (owner != shard)
    every_block = jnp.arange(shards * per_shard, dtype=jnp.int32)
    matches = flat[:, None] == every_block[None, :]
    present = jnp.any(matches & remote[:, None], axis=0).astype(jnp.int32).reshape(shards, per_shard)
    rank = jnp.cumsum(present, axis=1)
    wanted_rank = jnp.arange(1, CAP + 1, dtype=jnp.int32)[None, :, None]
    slot_hit = present[:, None, :] * (rank[:, None, :] == wanted_rank).astype(jnp.int32)
    requests = (
        jnp.sum(slot_hit * jnp.arange(per_shard, dtype=jnp.int32)[None, None, :], axis=2)
        + jnp.sum(slot_hit, axis=2)
        - 1
    )
    incoming = lax.all_to_all(requests, "seq", split_axis=0, concat_axis=0, tiled=True)
    slot_rank = jnp.sum(matches.astype(jnp.int32) * rank.reshape(-1)[None, :], axis=1)
    table_index = jnp.where(
        owner == shard, flat - shard * per_shard, per_shard + owner * CAP + slot_rank - 1
    )
    table_index = jnp.where(flat >= 0, table_index, 0)
    incoming_index = jnp.where(incoming >= 0, incoming, per_shard).reshape(-1)

    picked = table[jnp.maximum(flat, 0)]
    keys = lax.all_to_all(
        picked.reshape(members, groups_mine * select, part_len, latent), "vocab", 0, 0, tiled=True
    )

    mine = lax.dynamic_slice_in_dim(block_lists, member * groups_mine, groups_mine, 0)
    part_start = jnp.arange(members, dtype=jnp.int32) * part_len
    start = jnp.where(
        mine[:, None, :] >= 0, mine[:, None, :] * block_len + part_start[None, :, None], 1 << 30
    ).reshape(groups_mine, members * select)
    first = shard * (per_shard * block_len) + per_shard * block_len - rows + member * groups_mine * qgroup
    grad_q, grad_keys = attention(start, first.reshape(1), q, d, keys, groups_mine)

    entries = lax.all_to_all(grad_keys, "vocab", 0, 0, tiled=True)
    grad_query = lax.all_to_all(grad_q, "vocab", 0, 0, tiled=True).reshape(rows, heads, latent)
    local, outgoing = sum_by_block(
        table_index, entries.reshape(groups * select, part_len, latent), per_shard, slots
    )
    arrived = lax.all_to_all(
        outgoing.reshape(shards, CAP, part_len, latent), "seq", 0, 0, tiled=True
    ).reshape(slots, part_len, latent)
    grad_cache = receive(incoming_index, arrived, local)
    return grad_query, grad_cache


def solution(mesh):
    in_specs = (
        P("seq", "vocab", None),
        P("seq", None, None),
        P("seq", None),
        P("seq", "vocab", None),
    )
    out_specs = (P("seq", "vocab", None), P("seq", "vocab", None))
    return jax.shard_map(body, mesh=mesh, in_specs=in_specs, out_specs=out_specs, check_vma=False)
```

time: 807 us -> 336 us (0.42)
  waiting for transfers between devices: 474 us -> 189 us
  local copies, waits for them, and re-layouts: 116 us -> 23 us
  matrix products: 92.8 us -> 0 us
  other arithmetic: 72.2 us -> 1.37 us
  Pallas kernels: 0 us -> 32.8 us
  starting transfers between devices: 14.5 us -> 36.4 us
  blocking collectives: 20.4 us -> 36.2 us
    all_to_all x2 -> x6, waiting for transfers between devices: 453 us -> 134 us  [the longest x1 54.8 us: body(): lax.all_to_all(outgoing.reshape(shards, CAP, part_len, latent), 'seq', 0,...]
    dot_general x41 -> x0, matrix products: 92.8 us -> none  [the longest x8 25.6 us: one_group(): jnp.einsum('rhsk,rhl->skl', grad_low, query_group, preferred_element_type...]
    all_gather x0 -> x1, waiting for transfers between devices: none -> 54.7 us  [body(): table = lax.all_gather(quarter, 'seq', axis=0, tiled=True)]
    scatter-add x1 -> x0, other arithmetic: 45 us -> none  [body(): table_grad.at[table_index.reshape(-1)]]
    gather x9 -> x1, local copies, waits for them, and re-layouts: 48.4 us -> 6.33 us  [body(): picked = table[jnp.maximum(flat, 0)]]
    pallas_call x0 -> x3, Pallas kernels: none -> 32.8 us  [the longest x1 27.9 us: attention(): pl.pallas_call(attention_kernel, grid_spec=pltpu.PrefetchScalarGridSpec(n...]
    all_to_all x2 -> x6, starting transfers between devices: 14.3 us -> 36.4 us  [the longest x1 10.3 us: body(): lax.all_to_all(outgoing.reshape(shards, CAP, part_len, latent), 'seq', 0,...]
    reduce_scatter x1 -> x0, waiting for transfers between devices: 20.7 us -> none  [body(): lax.psum_scatter(owned, 'vocab', scatter_dimension=1, tiled=True)]
  transfers between devices with their start and end apart: 3 -> 7, of which waited for: 3 -> 5; matrix products, arithmetic and copies ran while one was open for 1% -> 6% of each run, Pallas kernels for 0% -> 9%
where the time goes in v1:
time: 336 us; the launch traced here: 333 us
  waiting for transfers between devices  189 us (56%)
  starting transfers between devices  36.4 us (11%)
  blocking collectives  36.2 us (11%)
  Pallas kernels  32.8 us (10%)
  local copies, waits for them, and re-layouts  23 us (7%)
  between operations  14.2 us (4%)
    all_to_all x1, waiting for transfers between devices, body(): lax.all_to_all(outgoing.reshape(shards, CAP, part_len, latent), 'seq', 0,...  54.8 us
    all_gather x1, waiting for transfers between devices, body(): table = lax.all_gather(quarter, 'seq', axis=0, tiled=True)  54.7 us
    all_to_all x1, blocking collectives, body(): entries = lax.all_to_all(grad_keys, 'vocab', 0, 0, tiled=True)  36.2 us
    all_to_all x1, waiting for transfers between devices, body(): lax.all_to_all(picked.reshape(members, groups_mine * select, part_len, la...  30.9 us
    pallas_call x1, Pallas kernels, attention(): pl.pallas_call(attention_kernel, grid_spec=pltpu.PrefetchScalarGridSpec(n...  27.9 us
    all_to_all x1, waiting for transfers between devices, body(): lax.all_to_all(grad_q, 'vocab', 0, 0, tiled=True)  26.9 us
    all_to_all x1, waiting for transfers between devices, body(): lax.all_to_all(d_out.reshape(members, rows // members, heads, value), 'vo...  21.4 us
    unnamed x12, local copies, waits for them, and re-layouts  13.8 us
  transfers between devices with their start and end apart: 7, of which 5 were waited for; matrix products, arithmetic and copies ran while one was open for 6% of the time, Pallas kernels for 9%

profile of v1, /device:TPU:2, one launch (start us, length us, event | category | flops | bytes accessed | tf_op | source)
XLA Modules:
  0.0 332.6 jit_solution(13239311195115731975)
XLA Ops:
  7.2 0.0 copy-start
  7.2 0.0 all-gather.2.cloned.1.call-start
  7.2 1.0 copy-done
  8.3 0.7 constant_dynamic-slice_fusion
  8.9 0.0 all-gather.2.cloned.1.call-update
  9.0 4.5 %all-to-all-start.1 = ((bf16[4,32,16,512]{3,2,1,0:T(8,128)(2,1)}), bf16[4,32,16,512]{3,2,1,0:T(8,128)(2,1)S(1)}, u32[]{:S(2)}, u32[]{:S(2)}) async-start(bf16[4,32,16,512]{3,2,1,0:T(8,128)(2,1)} %bitcast.15), calls=%async_computation.1 | async-start | bytes 4194304 | tf_op jit(solution)/shard_map/all_to_all | solution.py:177
  13.4 4.9 %copy.15 = bf16[128,16,576]{2,1,0:T(8,128)(2,1)} copy(bf16[128,16,576]{0,2,1:T(8,128)(2,1)} %param.4) | data formatting | bytes 4718592 | tf_op args[0]
  18.3 21.4 %all-to-all-done.1.d_ref = bf16[4,32,16,512]{3,2,1,0:T(8,128)(2,1)S(1)} async-done(((bf16[4,32,16,512]{3,2,1,0:T(8,128)(2,1)}), bf16[4,32,16,512]{3,2,1,0:T(8,128)(2,1)S(1)}, u32[]{:S(2)}, u32[]{:S(2)}) %all-to-all-start.1) | async-done | bytes 2097184 | tf_op jit(solution)/shard_map/all_to_all | solution.py:177
  39.8 0.0 copy-start.4
  39.8 4.7 %all-to-all-start = ((bf16[4,32,16,576]{3,2,1,0:T(8,128)(2,1)}), bf16[4,32,16,576]{3,2,1,0:T(8,128)(2,1)}, u32[]{:S(2)}, u32[]{:S(2)}) async-start(bf16[4,32,16,576]{3,2,1,0:T(8,128)(2,1)} %bitcast.14), calls=%async_computation | async-start | bytes 5242880 | tf_op jit(solution)/shard_map/all_to_all | solution.py:174
  44.5 0.0 copy-done.4
  44.5 0.1 reshape.136
  44.6 54.7 %all-gather.2.cloned.1.call-done = bf16[512,16,576]{2,1,0:T(8,128)(2,1)} async-done(((bf16[8,16,576]{2,1,0:T(8,128)(2,1)}), bf16[512,16,576]{2,1,0:T(8,128)(2,1)}) %all-gather.2.cloned.1.call-update) | async-done | bytes 9437200 | tf_op jit(solution)/shard_map/all_gather | solution.py:172
  99.2 6.3 %gather_fusion = bf16[128,16,576]{2,1,0:T(8,128)(2,1)} fusion(bf16[512,16,576]{2,1,0:T(8,128)(2,1)} %all-gather.2.cloned.1.call-done, s32[1024]{0:T(1024)S(1)} %pad_clamp_fusion), kind=kCustom, calls=%fused_computation | custom fusion | bytes 4719104 | tf_op jit(solution)/shard_map/gather | solution.py:203
  105.6 0.0 all-to-all-done.q_ref
  105.6 4.5 %all-to-all-start.2 = ((bf16[4,32,16,576]{3,2,1,0:T(8,128)(2,1)}), bf16[4,32,16,576]{3,2,1,0:T(8,128)(2,1)}, u32[]{:S(2)}, u32[]{:S(2)}) async-start(bf16[4,32,16,576]{3,2,1,0:T(8,128)(2,1)} %bitcast.13), calls=%async_computation.2 | async-start | bytes 5242880 | tf_op jit(solution)/shard_map/all_to_all | solution.py:204
  110.1 0.1 eq.32
  110.2 0.1 fusion.1
  110.4 0.1 reshape.133
  110.5 0.2 reduce_window_sum.11
  110.6 0.1 copy.17
  110.7 0.1 add.77
  110.8 0.1 broadcast_in_dim.31
  110.9 0.1 add.78
  111.0 0.1 add.79
  111.1 0.1 copy.16
  111.1 0.1 select_reduce_fusion.1
  111.2 0.7 copy.18
  112.0 30.9 %all-to-all-done.2.k_ref = bf16[4,32,16,576]{3,2,1,0:T(8,128)(2,1)} async-done(((bf16[4,32,16,576]{3,2,1,0:T(8,128)(2,1)}), bf16[4,32,16,576]{3,2,1,0:T(8,128)(2,1)}, u32[]{:S(2)}, u32[]{:S(2)}) %all-to-all-start.2) | async-done | bytes 2359328 | tf_op jit(solution)/shard_map/all_to_all | solution.py:204
  142.8 7.8 %all-to-all-start.4 = ((s32[64,1,2]{2,1,0:T(1,128)}), s32[64,1,2]{2,1,0:T(1,128)S(1)}, u32[]{:S(2)}, u32[]{:S(2)}) async-start(s32[64,1,2]{2,1,0:T(1,128)} %copy.18), calls=%async_computation.4 | async-start | bytes 65536 | tf_op jit(solution)/shard_map/all_to_all | solution.py:195
  150.6 27.9 %shard_map.59 = (bf16[4,32,16,576]{3,2,1,0:T(8,128)(2,1)}, bf16[4,32,16,576]{3,2,1,0:T(8,128)(2,1)}) custom-call(s32[2,64]{1,0:T(2,128)S(1)} %add_select_fusion.start_ref, s32[1]{0:T(128)} %bitcast.first_ref, bf16[4,32,16,576]{3,2,1,0:T(8,128)(2,1)} %all-to-all-done.q_ref, bf16[4,32,16,512]{3,2,1,0:T(8,128)(2,1)S(1)} %all-to-all-done.1.d_ref, ...), custom_call_target="tpu_custom_call" | custom-call | flops 11542724608 | bytes 16777216 | tf_op jit(solution)/shard_map/pallas_call | solution.py:72
  178.6 0.0 all-to-all-done.4
  178.6 36.2 %all_to_all.39 = bf16[4,32,16,576]{3,2,1,0:T(8,128)(2,1)S(1)} all-to-all(bf16[4,32,16,576]{3,2,1,0:T(8,128)(2,1)} %get-tuple-element.7), channel_id=1, replica_groups=mesh['seq'=64,'vocab'=4] {'vocab'}, dimensions={0} | all-to-all | bytes 4718592 | tf_op jit(solution)/shard_map/all_to_all | solution.py:216
  214.7 4.5 %all-to-all-start.3 = ((bf16[4,32,16,576]{3,2,1,0:T(8,128)(2,1)}), bf16[4,32,16,576]{3,2,1,0:T(8,128)(2,1)}, u32[]{:S(2)}, u32[]{:S(2)}) async-start(bf16[4,32,16,576]{3,2,1,0:T(8,128)(2,1)} %get-tuple-element.6), calls=%async_computation.3 | async-start | bytes 5242880 | tf_op jit(solution)/shard_map/all_to_all | solution.py:217
  219.3 0.1 mul.76
  219.4 0.2 select_reduce_fusion
  219.6 2.3 shard_map.60
  221.9 0.0 copy-start.1
  221.9 1.5 copy-done.1
  223.4 0.0 copy-start.2
  223.4 0.7 copy-done.2
  224.1 26.9 %all-to-all-done.3 = bf16[4,32,16,576]{3,2,1,0:T(8,128)(2,1)} async-done(((bf16[4,32,16,576]{3,2,1,0:T(8,128)(2,1)}), bf16[4,32,16,576]{3,2,1,0:T(8,128)(2,1)}, u32[]{:S(2)}, u32[]{:S(2)}) %all-to-all-start.3) | async-done | bytes 2359328 | tf_op jit(solution)/shard_map/all_to_all | solution.py:217
  251.0 10.3 %all-to-all-start.6 = ((bf16[64,2,16,576]{3,2,1,0:T(8,128)(2,1)}), bf16[64,2,16,576]{3,2,1,0:T(8,128)(2,1)S(1)}, u32[]{:S(2)}, u32[]{:S(2)}) async-start(bf16[64,2,16,576]{3,2,1,0:T(8,128)(2,1)} %bitcast.12), calls=%async_computation.6 | async-start | bytes 5242880 | tf_op jit(solution)/shard_map/all_to_all | solution.py:221
  261.4 0.5 broadcast.133
  261.9 0.7 reduce.3
  262.6 0.1 all_to_all.29
  262.8 4.7 %copy.19 = bf16[128,16,576]{0,2,1:T(8,128)(2,1)} copy(bf16[128,16,576]{2,1,0:T(8,128)(2,1)} %bitcast.4) | data formatting | bytes 4718592
  267.4 54.8 %all-to-all-done.6 = bf16[64,2,16,576]{3,2,1,0:T(8,128)(2,1)S(1)} async-done(((bf16[64,2,16,576]{3,2,1,0:T(8,128)(2,1)}), bf16[64,2,16,576]{3,2,1,0:T(8,128)(2,1)S(1)}, u32[]{:S(2)}, u32[]{:S(2)}) %all-to-all-start.6) | async-done | bytes 2359328 | tf_op jit(solution)/shard_map/all_to_all | solution.py:221
  322.3 0.0 copy-start.3
  322.3 1.0 copy-done.3
  323.2 2.5 shard_map.61
  (14 shorter events, 0.1 us)
Async XLA Ops:
  7.2 1.1 copy-start
  7.2 92.1 %all-gather.2.cloned.1.call-start = ((), (), s32[]{:S(2)}) async-start(), calls=%async_computation.7 | async-start | bytes 10649600 | tf_op jit(solution)/shard_map/all_gather | solution.py:172
  9.0 30.8 %all-to-all-start.1 = ((bf16[4,32,16,512]{3,2,1,0:T(8,128)(2,1)}), bf16[4,32,16,512]{3,2,1,0:T(8,128)(2,1)S(1)}, u32[]{:S(2)}, u32[]{:S(2)}) async-start(bf16[4,32,16,512]{3,2,1,0:T(8,128)(2,1)} %bitcast.15), calls=%async_computation.1 | async-start | bytes 4194304 | tf_op jit(solution)/shard_map/all_to_all | solution.py:177
  39.8 4.7 %copy-start.4 = (s32[8,16]{1,0:T(8,128)S(1)}, s32[8,16]{1,0:T(8,128)}, u32[]{:S(2)}) copy-start(s32[8,16]{1,0:T(8,128)} %param.6) | copy-start | bytes 1540
  39.8 65.8 %all-to-all-start = ((bf16[4,32,16,576]{3,2,1,0:T(8,128)(2,1)}), bf16[4,32,16,576]{3,2,1,0:T(8,128)(2,1)}, u32[]{:S(2)}, u32[]{:S(2)}) async-start(bf16[4,32,16,576]{3,2,1,0:T(8,128)(2,1)} %bitcast.14), calls=%async_computation | async-start | bytes 5242880 | tf_op jit(solution)/shard_map/all_to_all | solution.py:174
  105.6 37.3 %all-to-all-start.2 = ((bf16[4,32,16,576]{3,2,1,0:T(8,128)(2,1)}), bf16[4,32,16,576]{3,2,1,0:T(8,128)(2,1)}, u32[]{:S(2)}, u32[]{:S(2)}) async-start(bf16[4,32,16,576]{3,2,1,0:T(8,128)(2,1)} %bitcast.13), calls=%async_computation.2 | async-start | bytes 5242880 | tf_op jit(solution)/shard_map/all_to_all | solution.py:204
  142.8 35.7 %all-to-all-start.4 = ((s32[64,1,2]{2,1,0:T(1,128)}), s32[64,1,2]{2,1,0:T(1,128)S(1)}, u32[]{:S(2)}, u32[]{:S(2)}) async-start(s32[64,1,2]{2,1,0:T(1,128)} %copy.18), calls=%async_computation.4 | async-start | bytes 65536 | tf_op jit(solution)/shard_map/all_to_all | solution.py:195
  214.7 36.3 %all-to-all-start.3 = ((bf16[4,32,16,576]{3,2,1,0:T(8,128)(2,1)}), bf16[4,32,16,576]{3,2,1,0:T(8,128)(2,1)}, u32[]{:S(2)}, u32[]{:S(2)}) async-start(bf16[4,32,16,576]{3,2,1,0:T(8,128)(2,1)} %get-tuple-element.6), calls=%async_computation.3 | async-start | bytes 5242880 | tf_op jit(solution)/shard_map/all_to_all | solution.py:217
  221.9 1.5 copy-start.1
  223.4 0.7 copy-start.2
  251.0 71.2 %all-to-all-start.6 = ((bf16[64,2,16,576]{3,2,1,0:T(8,128)(2,1)}), bf16[64,2,16,576]{3,2,1,0:T(8,128)(2,1)S(1)}, u32[]{:S(2)}, u32[]{:S(2)}) async-start(bf16[64,2,16,576]{3,2,1,0:T(8,128)(2,1)} %bitcast.12), calls=%async_computation.6 | async-start | bytes 5242880 | tf_op jit(solution)/shard_map/all_to_all | solution.py:221
  322.3 1.0 copy-start.3
Sparse Core Ops, SparseCore 0:
  11.3 87.8 all-gather.1
